TPU v7x, 32 devices: a whole 2x2x4 slice. The times are simulated.
32 devices in a mesh: gz: 4 (over y, core), xy: 8 (over z, x).
Axes of the slice: x: 2, y: 2, z: 4, core: 2. Of those that a mesh axis runs over, the one named last changes fastest.
Arguments:
- cotangent: bfloat16 [4, 8, 9, 128, 128], P('gz', 'xy'), may hold values from -6 to 6
- displacement: float32 [4, 8, 3, 32, 128], P('gz', 'xy'), may hold values from -2 to 2
- neighbours: int32 [4, 8, 32, 128], P('gz', 'xy'), may hold values from 0 to 2303
- counts: int32 [4, 8, 128], P('gz', 'xy'), may hold values from 8 to 32, as said below
- atom_feat: bfloat16 [4, 8, 256, 128], P('gz', 'xy'), may hold values from -6 to 6
- radial_weight: float32 [3, 16, 128], replicated, may hold values from -1.5 to 1.5
- mix_weight: bfloat16 [3, 128, 128], replicated, may hold values from -0.5 to 0.5
Outputs:
- atom_grad: float32 [4, 8, 256, 128], P('gz', 'xy')
- radial_grad: float32 [3, 16, 128], replicated
- mix_grad: float32 [3, 128, 128], replicated
Inputs may be any that keep to these rules, and one draw needn't show every extreme that they name: `counts`: the first probe of the first brick uses all 32 slots and the first probe of the second brick uses 32 // 4.
All inputs are finite; a program needn't handle non-finite values.
Results may differ from a plain program's by a relative error of at most 0.0051.
Values may be sent and summed in bfloat16 or wider, within the bound.
A program may use at most 64 MiB of HBM per device.

v0:
```python
import math
import jax
import jax.numpy as jnp
from jax import lax
from jax.sharding import PartitionSpec as P

CUTOFF = 4.0
LEVEL_SPANS = ((0, 1), (1, 4), (4, 9))


def padded(cells, sides, width):
    for axis, dim in sides:
        count = lax.axis_size(axis)
        head = lax.slice_in_dim(cells, 0, width, axis=dim)
        tail = lax.slice_in_dim(cells, cells.shape[dim] - width, cells.shape[dim], axis=dim)
        cells = jnp.concatenate(
            [
                lax.ppermute(tail, axis, [(i, (i + 1) % count) for i in range(count)]),
                cells,
                lax.ppermute(head, axis, [((i + 1) % count, i) for i in range(count)]),
            ],
            axis=dim,
        )
    return cells


def harmonics(disp):
    scaled = disp / CUTOFF
    coord_x, coord_y, coord_z = (scaled[0], scaled[1], scaled[2])
    root3, root5, root15 = (math.sqrt(3.0), math.sqrt(5.0), math.sqrt(15.0))
    return jnp.stack(
        [
            jnp.ones_like(coord_x),
            root3 * coord_x,
            root3 * coord_y,
            root3 * coord_z,
            root15 * coord_x * coord_y,
            root15 * coord_y * coord_z,
            0.5 * root5 * (2.0 * coord_z * coord_z - coord_x * coord_x - coord_y * coord_y),
            root15 * coord_x * coord_z,
            0.5 * root15 * (coord_x * coord_x - coord_y * coord_y),
        ]
    )


def basis(disp, nbasis):
    distance = jnp.sqrt(jnp.sum(disp * disp, axis=0))
    centres = jnp.arange(nbasis).astype(jnp.float32) * (CUTOFF / (nbasis - 1))
    sharpness = ((nbasis - 1) / CUTOFF) ** 2
    envelope = 0.5 * (jnp.cos(math.pi * distance / CUTOFF) + 1.0)
    shaped = centres.reshape((nbasis,) + (1,) * distance.ndim)
    return jnp.exp(-sharpness * (distance[None] - shaped) ** 2) * envelope[None]


def exact(form, left, right):
    return jnp.einsum(form, left, right, precision=lax.Precision.HIGHEST)


def matmul(form, left, right):
    return jnp.einsum(form, left, right, preferred_element_type=jnp.float32)


def gate_backward(moments, mix_weight, cotangent):
    mixed_out = [
        matmul("mpc,cd->mpd", moments[span_start:span_end], mix_weight[level])
        for level, (span_start, span_end) in enumerate(LEVEL_SPANS)
    ]
    scalar = mixed_out[0][0]
    gating = jax.nn.sigmoid(scalar)
    gate_slope = gating * (1.0 - gating)
    cot_float = cotangent.astype(jnp.float32)
    higher = jnp.concatenate(mixed_out[1:], 0)
    first_term = (
        cot_float[0] * (gating + scalar * gate_slope)
        + jnp.sum(cot_float[1:] * higher, 0) * gate_slope
    )
    dmixed = jnp.concatenate([first_term[None], cot_float[1:] * gating[None]], 0).astype(
        jnp.bfloat16
    )
    dmoments = jnp.concatenate(
        [
            matmul("mpd,cd->mpc", dmixed[span_start:span_end], mix_weight[level])
            for level, (span_start, span_end) in enumerate(LEVEL_SPANS)
        ],
        0,
    ).astype(jnp.bfloat16)
    mix_part = jnp.stack(
        [
            matmul("mpc,mpd->cd", moments[span_start:span_end], dmixed[span_start:span_end])
            for span_start, span_end in LEVEL_SPANS
        ]
    )
    return (dmoments, mix_part)


def shards(cotangent, displacement, neighbours, counts, atom_feat, radial_weight, mix_weight):
    cot_local = cotangent[0, 0]
    disp_local = displacement[0, 0]
    neighbour_local_index = neighbours[0, 0]
    probe_tally = counts[0, 0]
    slot_count = neighbour_local_index.shape[0]
    probe_count = neighbour_local_index.shape[1]
    natom = atom_feat.shape[2]
    channels = atom_feat.shape[3]
    nbasis = radial_weight.shape[1]
    filled_slots = (
        lax.broadcasted_iota(jnp.int32, (slot_count, probe_count), 0) < probe_tally[None]
    ).astype(jnp.float32)
    angular = harmonics(disp_local) * filled_slots[None]
    radial_basis = basis(disp_local, nbasis)
    atom_table = padded(atom_feat, (("gz", 0), ("xy", 1)), 1).reshape(9 * natom, channels)
    features = atom_table[neighbour_local_index].astype(jnp.float32)
    radial = exact("bkp,lbc->lkpc", radial_basis, radial_weight)
    pieces = []
    for level, (span_start, span_end) in enumerate(LEVEL_SPANS):
        weighted = radial[level] * features
        pieces.append(jnp.sum(angular[span_start:span_end, :, :, None] * weighted[None], axis=1))
    moments = jnp.concatenate(pieces, 0).astype(jnp.bfloat16)
    dmoments, mix_part = gate_backward(moments, mix_weight, cot_local)
    mix_total = lax.psum(mix_part, ("gz", "xy"))
    dmoment_float = dmoments.astype(jnp.float32)
    contrib = jnp.zeros(features.shape, jnp.float32)
    radial_parts = []
    for level, (span_start, span_end) in enumerate(LEVEL_SPANS):
        traced = jnp.sum(
            angular[span_start:span_end, :, :, None] * dmoment_float[span_start:span_end, None],
            axis=0,
        )
        contrib = contrib + radial[level] * traced
        radial_parts.append(exact("bkp,kpc->bc", radial_basis, features * traced))
    grads = (
        jnp.zeros((9 * natom, channels), jnp.float32)
        .at[neighbour_local_index.reshape(-1)]
        .add(contrib.reshape(-1, channels))
    )
    radial_part = jnp.stack(radial_parts)
    radial_total = lax.psum(radial_part, ("gz", "xy"))
    blocks = grads.reshape(3, 3, natom, channels)
    outer_rows = jnp.stack([blocks[0], blocks[2]], 0)
    arrived = padded(outer_rows, (("gz", 0),), 1)
    columns = blocks[1] + arrived[0] + arrived[3]
    outer_columns = jnp.stack([columns[0], columns[2]], 0)
    landed = padded(outer_columns, (("xy", 0),), 1)
    owned = columns[1] + landed[0] + landed[3]
    return (owned[None, None], radial_total, mix_total)


def solution(mesh):
    in_specs = (
        P("gz", "xy", None, None, None),
        P("gz", "xy", None, None, None),
        P("gz", "xy", None, None),
        P("gz", "xy", None),
        P("gz", "xy", None, None),
        P(),
        P(),
    )
    out_specs = (P("gz", "xy", None, None), P(), P())
    return jax.shard_map(shards, mesh=mesh, in_specs=in_specs, out_specs=out_specs, check_vma=False)
```

profile of v0, /device:TPU:10, one launch (start us, length us, event | category | flops | bytes accessed | tf_op | source)
XLA Modules:
  0.0 237.2 jit_solution(9430039311791269466)
XLA Ops:
  7.3 1.7 collective-permute-start.1
  9.0 0.8 multiply_reduce_fusion.5
  9.9 0.7 fusion.78
  10.7 1.3 compare_select_fusion
  12.1 7.2 %convolution_bitcast_fusion = f32[3,32,128,128]{3,2,0,1:T(8,128)} fusion(f32[32,128]{1,0:T(8,128)S(1)} %get-tuple-element.23, f32[16]{0:T(128)S(1)} %convert_multiply_fusion, f32[32,128]{1,0:T(8,128)S(1)} %get-tuple-element.22, f32[3,16,128]{2,1,0:T(8,128)S(1)} %copy-done), kind=kOutput, calls=%fused_computation.6 | convolution fusion | flops 302252032 | bytes 6348864 | tf_op jit(solution)/shard_map/bkp,lbc->lkpc/dot_general | solution.py:56
  19.4 0.9 convert_element_type.43
  20.3 1.6 collective-permute-start.2
  21.9 0.5 collective-permute-start.3
  22.4 8.9 %collective-permute-done.2 = bf16[3,1,256,128]{3,2,1,0:T(8,128)(2,1)S(1)} collective-permute-done((bf16[3,1,256,128]{3,2,1,0:T(8,128)(2,1)S(1)}, bf16[3,1,256,128]{3,2,1,0:T(8,128)(2,1)S(1)}, u32[]{:S(2)}, u32[]{:S(2)}) %collective-permute-start.2) | collective-permute-done | bytes 196640 | tf_op jit(solution)/shard_map/ppermute | solution.py:18
  31.4 12.1 %gather_fusion = bf16[4096,128]{1,0:T(8,128)(2,1)S(1)} fusion(bf16[2304,128]{1,0:T(8,128)(2,1)S(1)} %bitcast.167, s32[4096]{0:T(1024)S(1)} %fusion.74), kind=kCustom, calls=%fused_computation | custom fusion | bytes 2113536 | tf_op jit(solution)/shard_map/gather | solution.py:112
  43.7 3.6 %fusion.83 = (f32[1,32,128,128]{3,2,0,1:T(8,128)S(1)}, bf16[128,128]{1,0:T(8,128)(2,1)S(1)}, f32[32,128,128]{2,1,0:T(8,128)S(1)}, f32[32,128,128]{2,1,0:T(8,128)...) fusion(f32[3,32,128,128]{3,2,0,1:T(8,128)} %convolution_bitcast_fusion, ...), kind=kLoop, calls=%fused_computation.141 | loop fusion | flops 3129344 | bytes 19972096 | tf_op jit(solution)/shard_map/slice | solution.py:129
  47.3 2.0 multiply_reduce_fusion.3
  49.4 3.1 %multiply_reduce_fusion.1 = bf16[5,128,128]{2,1,0:T(8,128)(2,1)S(1)} fusion(f32[32,128,128]{2,1,0:T(8,128)S(1)} %get-tuple-element.7, f32[5,32,128]{2,1,0:T(8,128)S(1)} %slice.162), kind=kLoop, calls=%fused_computation.3 | loop fusion | flops 5160960 | bytes 2342912 | tf_op jit(solution)/shard_map/reduce_sum | solution.py:117
  53.0 0.2 convolution_bitcast_fusion.2
  53.2 0.2 convolution_bitcast_fusion.1
  53.5 0.2 convolution_convert_fusion
  54.1 2.1 multiply_reduce_fusion.2
  56.3 2.1 fusion.11
  58.4 2.0 fusion.14
  60.4 3.2 %multiply_reduce_fusion = f32[32,128,128]{2,1,0:T(8,128)S(1)} fusion(f32[5,128,128]{2,1,0:T(8,128)S(1)} %fusion.27, f32[5,32,128]{2,1,0:T(8,128)S(1)} %slice.162), kind=kLoop, calls=%fused_computation.2 | loop fusion | flops 4718592 | bytes 2506752 | tf_op jit(solution)/shard_map/reduce_sum | solution.py:125
  63.6 2.4 %fusion = f32[4096,128]{1,0:T(8,128)} fusion(f32[32,128,128]{2,1,0:T(8,128)S(1)} %multiply_reduce_fusion, f32[1,32,128,128]{3,2,0,1:T(8,128)S(1)} %get-tuple-element.9, f32[32,128,128]{2,1,0:T(8,128)S(1)} %multiply_reduce_fusion.2, f32[1,32,128,128]{3,2,0,1:T(8,128)S(1)} %get-tuple-element.10, f32[1,32,128,128]{3,2,0,1:T(8,128)S(1)} %get-tuple-element.5, ...), kind=kLoop, calls=%fused_computation.8 | loop fusion | flops 3145728 | bytes 12664832 | tf_op jit(solution)/shard_map/add | solution.py:129
  66.1 22.9 %scatter_custom_fusion = f32[2304,128]{1,0:T(8,128)S(1)} fusion(s32[4096]{0:T(1024)} %bitcast.176, f32[4096,128]{1,0:T(8,128)} %fusion, f32[]{:T(128)} %constant.14.clone.1), kind=kCustom, calls=%fused_computation.36 | custom fusion | flops 524288 | bytes 1180160 | tf_op jit(solution)/shard_map/scatter-add | solution.py:134
  89.2 1.7 collective-permute-start.5
  90.9 0.2 convolution_bitcast_fusion.3
  91.1 1.3 fusion.17
  92.5 7.3 %collective-permute-done.4 = f32[1,3,256,128]{3,2,1,0:T(8,128)S(1)} collective-permute-done((f32[1,3,256,128]{3,2,1,0:T(8,128)S(1)}, f32[1,3,256,128]{3,2,1,0:T(8,128)S(1)}, u32[]{:S(2)}, u32[]{:S(2)}) %collective-permute-start.4) | collective-permute-done | bytes 393248 | tf_op jit(solution)/shard_map/ppermute | solution.py:18
  99.9 2.5 %collective-permute-start.6 = (f32[1,256,128]{2,1,0:T(8,128)S(1)}, f32[1,256,128]{2,1,0:T(8,128)S(1)}, u32[]{:S(2)}, u32[]{:S(2)}) collective-permute-start(f32[1,256,128]{2,1,0:T(8,128)S(1)} %get-tuple-element.16), channel_id=1, source_target_pairs={{0,1},{1,2},{2,3},{3,4},{4,5},{5,6},{6,7},{7,0},{8,9},{9,10},{10,1... | collective-permute-start | bytes 393224 | tf_op jit(solution)/shard_map/ppermute | solution.py:18
  102.4 0.7 pad_maximum_fusion.1
  103.1 43.0 %psum.14 = f32[3,16,128]{2,1,0:T(8,128)} all-reduce(f32[3,16,128]{2,1,0:T(8,128)S(1)} %pad_maximum_fusion.4), channel_id=1, replica_groups=mesh['gz'=4,'xy'=8] {'gz','xy'}, use_global_device_ids=true, to_apply=%region_8.0 | all-reduce | flops 6144 | bytes 49152 | tf_op jit(solution)/shard_map/psum | solution.py:137
  146.1 0.7 fusion.29
  146.8 81.9 %all-reduce.2.cloned.1.call-done = f32[3,128,128]{2,1,0:T(8,128)} async-done(((f32[3,128,128]{2,1,0:T(8,128)}), f32[3,128,128]{2,1,0:T(8,128)}) %all-reduce.2.cloned.1.call-update) | async-done | bytes 196624 | tf_op jit(solution)/shard_map/psum | solution.py:120
  228.7 1.6 copy.28
  (72 shorter events, 1.8 us)
Async XLA Ops:
  7.2 4.9 %copy-start = (f32[3,16,128]{2,1,0:T(8,128)S(1)}, f32[3,16,128]{2,1,0:T(8,128)}, u32[]{:S(2)}) copy-start(f32[3,16,128]{2,1,0:T(8,128)} %param.12) | copy-start | bytes 73732
  7.2 221.5 %all-reduce.2.cloned.1.call-start = ((), (), s32[]{:S(2)}) async-start(), calls=%async_computation | async-start | bytes 393216 | tf_op jit(solution)/shard_map/psum | solution.py:120
  7.2 13.0 %collective-permute-start = (bf16[1,1,256,128]{3,2,1,0:T(8,128)(2,1)}, bf16[1,1,256,128]{3,2,1,0:T(8,128)(2,1)S(1)}, u32[]{:S(2)}, u32[]{:S(2)}) collective-permute-start(bf16[1,1,256,128]{3,2,1,0:T(8,128)(2,1)} %param.11), channel_id=1, source_target_pairs={{0,8},{8,16},{16,24},{24,0},{1,9},{9,17},{17,25},{25,1},{2,10},{10... | collective-permute-start | bytes 196616 | tf_op jit(solution)/shard_map/ppermute | solution.py:18
  7.3 13.0 %collective-permute-start.1 = (bf16[1,1,256,128]{3,2,1,0:T(8,128)(2,1)}, bf16[1,1,256,128]{3,2,1,0:T(8,128)(2,1)S(1)}, u32[]{:S(2)}, u32[]{:S(2)}) collective-permute-start(bf16[1,1,256,128]{3,2,1,0:T(8,128)(2,1)} %param.11), channel_id=1, source_target_pairs={{8,0},{16,8},{24,16},{0,24},{9,1},{17,9},{25,17},{1,25},{10,2},{18... | collective-permute-start | bytes 196616 | tf_op jit(solution)/shard_map/ppermute | solution.py:20
  9.0 47.2 %copy-start.11 = (f32[16]{0:T(128)}, f32[16]{0:T(128)S(1)}, u32[]{:S(2)}) copy-start(f32[16]{0:T(128)S(1)} %convert_multiply_fusion) | copy-start | bytes 196
  12.1 7.3 %copy-start.4 = (bf16[1,1,9,128,128]{4,3,2,1,0:T(8,128)(2,1)S(1)}, bf16[1,1,9,128,128]{4,3,2,1,0:T(8,128)(2,1)}, u32[]{:S(2)}) copy-start(bf16[1,1,9,128,128]{4,3,2,1,0:T(8,128)(2,1)} %param.7) | copy-start | bytes 884740
  12.1 8.2 %copy-start.6 = (bf16[1,1,256,128]{3,2,1,0:T(8,128)(2,1)S(1)}, bf16[1,1,256,128]{3,2,1,0:T(8,128)(2,1)}, u32[]{:S(2)}) copy-start(bf16[1,1,256,128]{3,2,1,0:T(8,128)(2,1)} %param.11) | copy-start | bytes 196612
  12.1 10.3 %copy-start.7 = (s32[1,1,32,128]{3,2,1,0:T(8,128)S(1)}, s32[1,1,32,128]{3,2,1,0:T(8,128)}, u32[]{:S(2)}) copy-start(s32[1,1,32,128]{3,2,1,0:T(8,128)} %param.9) | copy-start | bytes 49156
  19.3 24.3 %copy-start.8 = (f32[32,128]{1,0:T(8,128)}, f32[32,128]{1,0:T(8,128)S(1)}, u32[]{:S(2)}) copy-start(f32[32,128]{1,0:T(8,128)S(1)} %get-tuple-element.19) | copy-start | bytes 49156
  20.3 11.0 %collective-permute-start.2 = (bf16[3,1,256,128]{3,2,1,0:T(8,128)(2,1)S(1)}, bf16[3,1,256,128]{3,2,1,0:T(8,128)(2,1)S(1)}, u32[]{:S(2)}, u32[]{:S(2)}) collective-permute-start(bf16[3,1,256,128]{3,2,1,0:T(8,128)(2,1)S(1)} %constant_dynamic-update-slice_fusion.9), channel_id=1, source_target_pairs={{0,1},{1,2},{2,3},{3,4},{4,5},{5,6},{6,7},{7,0},{8,9},{9,10},{10,1... | collective-permute-start | bytes 589832 | tf_op jit(solution)/shard_map/ppermute | solution.py:18
  21.9 9.4 %collective-permute-start.3 = (bf16[3,1,256,128]{3,2,1,0:T(8,128)(2,1)S(1)}, bf16[3,1,256,128]{3,2,1,0:T(8,128)(2,1)S(1)}, u32[]{:S(2)}, u32[]{:S(2)}) collective-permute-start(bf16[3,1,256,128]{3,2,1,0:T(8,128)(2,1)S(1)} %constant_dynamic-update-slice_fusion.9), channel_id=1, source_target_pairs={{1,0},{2,1},{3,2},{4,3},{5,4},{6,5},{7,6},{0,7},{9,8},{10,9},{11,1... | collective-permute-start | bytes 589832 | tf_op jit(solution)/shard_map/ppermute | solution.py:20
  47.3 2.0 copy-start.5
  49.3 3.6 %copy-start.3 = (f32[1,1,9,128,128]{4,3,2,1,0:T(8,128)S(1)}, f32[1,1,9,128,128]{4,3,2,1,0:T(8,128)}, u32[]{:S(2)}) copy-start(f32[1,1,9,128,128]{4,3,2,1,0:T(8,128)} %convert_element_type.43) | copy-start | bytes 1769476
  53.9 2.4 %copy-start.9 = (f32[32,128]{1,0:T(8,128)S(1)}, f32[32,128]{1,0:T(8,128)}, u32[]{:S(2)}) copy-start(f32[32,128]{1,0:T(8,128)} %copy-done.8) | copy-start | bytes 49156
  63.6 2.4 %copy-start.1 = (f32[32,128,128]{2,1,0:T(8,128)}, f32[32,128,128]{2,1,0:T(8,128)S(1)}, u32[]{:S(2)}) copy-start(f32[32,128,128]{2,1,0:T(8,128)S(1)} %multiply_reduce_fusion) | copy-start | bytes 6291460
  66.1 25.0 %copy-start.12 = (f32[16]{0:T(128)S(1)}, f32[16]{0:T(128)}, u32[]{:S(2)}) copy-start(f32[16]{0:T(128)} %copy-done.11) | copy-start | bytes 196
  89.0 2.1 copy-start.2
  89.1 10.7 %collective-permute-start.4 = (f32[1,3,256,128]{3,2,1,0:T(8,128)S(1)}, f32[1,3,256,128]{3,2,1,0:T(8,128)S(1)}, u32[]{:S(2)}, u32[]{:S(2)}) collective-permute-start(f32[1,3,256,128]{3,2,1,0:T(8,128)S(1)} %bitcast.174), channel_id=1, source_target_pairs={{0,8},{8,16},{16,24},{24,0},{1,9},{9,17},{17,25},{25,1},{2,10},{10... | collective-permute-start | bytes 1179656 | tf_op jit(solution)/shard_map/ppermute | solution.py:18
  89.2 10.6 %collective-permute-start.5 = (f32[1,3,256,128]{3,2,1,0:T(8,128)S(1)}, f32[1,3,256,128]{3,2,1,0:T(8,128)S(1)}, u32[]{:S(2)}, u32[]{:S(2)}) collective-permute-start(f32[1,3,256,128]{3,2,1,0:T(8,128)S(1)} %bitcast.173), channel_id=1, source_target_pairs={{8,0},{16,8},{24,16},{0,24},{9,1},{17,9},{25,17},{1,25},{10,2},{18... | collective-permute-start | bytes 1179656 | tf_op jit(solution)/shard_map/ppermute | solution.py:20
  92.5 10.6 %copy-start.10 = (f32[1,16,128]{2,1,0:T(8,128)S(1)}, f32[1,16,128]{2,1,0:T(8,128)}, u32[]{:S(2)}) copy-start(f32[1,16,128]{2,1,0:T(8,128)} %fusion.11) | copy-start | bytes 24580
  99.9 46.2 %collective-permute-start.6 = (f32[1,256,128]{2,1,0:T(8,128)S(1)}, f32[1,256,128]{2,1,0:T(8,128)S(1)}, u32[]{:S(2)}, u32[]{:S(2)}) collective-permute-start(f32[1,256,128]{2,1,0:T(8,128)S(1)} %get-tuple-element.16), channel_id=1, source_target_pairs={{0,1},{1,2},{2,3},{3,4},{4,5},{5,6},{6,7},{7,0},{8,9},{9,10},{10,1... | collective-permute-start | bytes 393224 | tf_op jit(solution)/shard_map/ppermute | solution.py:18
  102.4 43.7 %collective-permute-start.7 = (f32[1,256,128]{2,1,0:T(8,128)S(1)}, f32[1,256,128]{2,1,0:T(8,128)S(1)}, u32[]{:S(2)}, u32[]{:S(2)}) collective-permute-start(f32[1,256,128]{2,1,0:T(8,128)S(1)} %get-tuple-element.17), channel_id=1, source_target_pairs={{1,0},{2,1},{3,2},{4,3},{5,4},{6,5},{7,6},{0,7},{9,8},{10,9},{11,1... | collective-permute-start | bytes 393224 | tf_op jit(solution)/shard_map/ppermute | solution.py:20
Sparse Core Ops, SparseCore 0:
  103.2 125.4 all-reduce.1
where the time goes:
time: 238 us; the launch traced here: 237 us
  waiting for transfers between devices  98.2 us (41%)
  other arithmetic  45.1 us (19%)
  blocking collectives  43 us (18%)
  between operations  14.5 us (6%)
  matrix products  14.3 us (6%)
  local copies, waits for them, and re-layouts  14 us (6%)
  starting transfers between devices  8.19 us (3%)
    psum x1, waiting for transfers between devices, shards(): mix_total = lax.psum(mix_part, ('gz', 'xy'))  81.9 us
    psum x1, blocking collectives, shards(): radial_total = lax.psum(radial_part, ('gz', 'xy'))  43 us
    scatter-add x1, other arithmetic, shards(): grads = jnp.zeros((9 * natom, channels), jnp.float32).at[neighbour_local_...  22.9 us
    ppermute x4, waiting for transfers between devices, padded(): lax.ppermute(tail, axis, [(i, (i + 1) % count) for i in range(count)])  16.2 us
    dot_general x4, matrix products, exact(): return jnp.einsum(form, left, right, precision=lax.Precision.HIGHEST)  12.7 us
    gather x1, local copies, waits for them, and re-layouts, shards(): features = atom_table[neighbour_local_index].astype(jnp.float32)  12.1 us
    reduce_sum x2, other arithmetic, shards(): jnp.sum(angular[span_start:span_end, :, :, None] * dmoment_float[span_sta...  5.34 us
    reduce_sum x2, other arithmetic, shards(): jnp.sum(angular[span_start:span_end, :, :, None] * weighted[None], axis=1)  5.1 us
  transfers between devices with their start and end apart: 9, of which 3 were waited for; matrix products, arithmetic and copies ran while one was open for 6% of the time, Pallas kernels for 0%

commit v1 on v0

--- a/solution.py
+++ b/solution.py
@@ -117,7 +117,7 @@
         pieces.append(jnp.sum(angular[span_start:span_end, :, :, None] * weighted[None], axis=1))
     moments = jnp.concatenate(pieces, 0).astype(jnp.bfloat16)
     dmoments, mix_part = gate_backward(moments, mix_weight, cot_local)
-    mix_total = lax.psum(mix_part, ("gz", "xy"))
+    mix_total = jnp.sum(lax.all_gather(mix_part, ("gz", "xy")), axis=0)
     dmoment_float = dmoments.astype(jnp.float32)
     contrib = jnp.zeros(features.shape, jnp.float32)
     radial_parts = []

time: 238 us -> 157 us (0.66)
  waiting for transfers between devices: 98.2 us -> 14.8 us
  other arithmetic: 45.1 us -> 49.1 us
    psum x1 -> x0, waiting for transfers between devices: 81.9 us -> none  [shards(): mix_total = lax.psum(mix_part, ('gz', 'xy'))]
    reduce_sum x0 -> x1, other arithmetic: none -> 3.78 us  [shards(): mix_total = jnp.sum(lax.all_gather(mix_part, ('gz', 'xy')), axis=0)]
  transfers between devices with their start and end apart: 9 -> 9, of which waited for: 3 -> 2; matrix products, arithmetic and copies ran while one was open for 6% -> 30% of each run, Pallas kernels for 0% -> 0%
where the time goes in v1:
time: 157 us; the launch traced here: 156 us
  other arithmetic  49.1 us (31%)
  blocking collectives  43.6 us (28%)
  waiting for transfers between devices  14.8 us (9%)
  between operations  14.5 us (9%)
  matrix products  13 us (8%)
  local copies, waits for them, and re-layouts  12.6 us (8%)
  starting transfers between devices  8.21 us (5%)
    psum x1, blocking collectives, shards(): radial_total = lax.psum(radial_part, ('gz', 'xy'))  43.6 us
    scatter-add x1, other arithmetic, shards(): grads = jnp.zeros((9 * natom, channels), jnp.float32).at[neighbour_local_...  23 us
    ppermute x4, waiting for transfers between devices, padded(): lax.ppermute(tail, axis, [(i, (i + 1) % count) for i in range(count)])  14.8 us
    gather x1, local copies, waits for them, and re-layouts, shards(): features = atom_table[neighbour_local_index].astype(jnp.float32)  12.1 us
    dot_general x4, matrix products, exact(): return jnp.einsum(form, left, right, precision=lax.Precision.HIGHEST)  11.3 us
    reduce_sum x2, other arithmetic, shards(): jnp.sum(angular[span_start:span_end, :, :, None] * dmoment_float[span_sta...  5.33 us
    reduce_sum x2, other arithmetic, shards(): jnp.sum(angular[span_start:span_end, :, :, None] * weighted[None], axis=1)  5.1 us
    slice x1, other arithmetic, shards(): contrib = contrib + radial[level] * traced  5.07 us
  transfers between devices with their start and end apart: 9, of which 2 were waited for; matrix products, arithmetic and copies ran while one was open for 30% of the time, Pallas kernels for 0%

profile of v1, /device:TPU:10, one launch (start us, length us, event | category | flops | bytes accessed | tf_op | source)
XLA Modules:
  0.0 155.8 jit_solution(9148573011479387827)
XLA Ops:
  7.3 1.7 %collective-permute-start.1 = (bf16[1,1,256,128]{3,2,1,0:T(8,128)(2,1)}, bf16[1,1,256,128]{3,2,1,0:T(8,128)(2,1)S(1)}, u32[]{:S(2)}, u32[]{:S(2)}) collective-permute-start(bf16[1,1,256,128]{3,2,1,0:T(8,128)(2,1)} %param.11), channel_id=1, source_target_pairs={{8,0},{16,8},{24,16},{0,24},{9,1},{17,9},{25,17},{1,25},{10,2},{18... | collective-permute-start | bytes 196616 | tf_op jit(solution)/shard_map/ppermute | solution.py:20
  9.0 0.8 multiply_reduce_fusion.5
  9.9 0.7 fusion.78
  10.8 7.2 %convolution_bitcast_fusion = f32[3,32,128,128]{3,2,0,1:T(8,128)} fusion(f32[32,128]{1,0:T(8,128)S(1)} %get-tuple-element.23, f32[16]{0:T(128)S(1)} %convert_multiply_fusion, f32[32,128]{1,0:T(8,128)S(1)} %get-tuple-element.22, f32[3,16,128]{2,1,0:T(8,128)S(1)} %copy-done), kind=kOutput, calls=%fused_computation.6 | convolution fusion | flops 302252032 | bytes 6348864 | tf_op jit(solution)/shard_map/bkp,lbc->lkpc/dot_general | solution.py:56
  18.0 0.9 convert_element_type.43
  19.0 1.6 %collective-permute-start.2 = (bf16[3,1,256,128]{3,2,1,0:T(8,128)(2,1)S(1)}, bf16[3,1,256,128]{3,2,1,0:T(8,128)(2,1)S(1)}, u32[]{:S(2)}, u32[]{:S(2)}) collective-permute-start(bf16[3,1,256,128]{3,2,1,0:T(8,128)(2,1)S(1)} %constant_dynamic-update-slice_fusion.9), channel_id=1, source_target_pairs={{0,1},{1,2},{2,3},{3,4},{4,5},{5,6},{6,7},{7,0},{8,9},{9,10},{10,1... | collective-permute-start | bytes 589832 | tf_op jit(solution)/shard_map/ppermute | solution.py:18
  20.6 0.5 collective-permute-start.3
  21.1 8.9 %collective-permute-done.2 = bf16[3,1,256,128]{3,2,1,0:T(8,128)(2,1)S(1)} collective-permute-done((bf16[3,1,256,128]{3,2,1,0:T(8,128)(2,1)S(1)}, bf16[3,1,256,128]{3,2,1,0:T(8,128)(2,1)S(1)}, u32[]{:S(2)}, u32[]{:S(2)}) %collective-permute-start.2) | collective-permute-done | bytes 196640 | tf_op jit(solution)/shard_map/ppermute | solution.py:18
  30.0 12.1 %gather_fusion = bf16[4096,128]{1,0:T(8,128)(2,1)S(1)} fusion(bf16[2304,128]{1,0:T(8,128)(2,1)S(1)} %bitcast.168, s32[4096]{0:T(1024)S(1)} %fusion.74), kind=kCustom, calls=%fused_computation | custom fusion | bytes 2113536 | tf_op jit(solution)/shard_map/gather | solution.py:112
  42.3 5.1 %fusion.83 = (f32[1,32,128,128]{3,2,0,1:T(8,128)}, bf16[128,128]{1,0:T(8,128)(2,1)S(1)}, f32[32,128,128]{2,1,0:T(8,128)S(1)}, f32[32,128,128]{2,1,0:T(8,128)S(1)...) fusion(f32[3,32,128,128]{3,2,0,1:T(8,128)} %convolution_bitcast_fusion, ...), kind=kLoop, calls=%fused_computation.141 | loop fusion | flops 3129344 | bytes 19972096 | tf_op jit(solution)/shard_map/slice | solution.py:129
  47.4 2.0 %multiply_reduce_fusion.3 = bf16[3,128,128]{2,1,0:T(8,128)(2,1)S(1)} fusion(f32[32,128,128]{2,1,0:T(8,128)S(1)} %get-tuple-element.8, f32[3,32,128]{2,1,0:T(8,128)S(1)} %slice.160), kind=kLoop, calls=%fused_computation.5 | loop fusion | flops 3096576 | bytes 2244608 | tf_op jit(solution)/shard_map/reduce_sum | solution.py:117
  49.5 3.1 %multiply_reduce_fusion.1 = bf16[5,128,128]{2,1,0:T(8,128)(2,1)S(1)} fusion(f32[32,128,128]{2,1,0:T(8,128)S(1)} %get-tuple-element.7, f32[5,32,128]{2,1,0:T(8,128)S(1)} %slice.162), kind=kLoop, calls=%fused_computation.3 | loop fusion | flops 5160960 | bytes 2342912 | tf_op jit(solution)/shard_map/reduce_sum | solution.py:117
  53.1 0.2 convolution_bitcast_fusion.2
  53.3 0.2 convolution_bitcast_fusion.1
  53.6 0.2 convolution_bitcast_fusion.3
  53.8 0.7 pad_maximum_fusion.1
  54.7 0.2 convolution_convert_fusion.1
  54.9 0.2 convolution_convert_fusion
  55.2 2.1 %multiply_reduce_fusion.2 = f32[32,128,128]{2,1,0:T(8,128)S(1)} fusion(f32[3,128,128]{2,1,0:T(8,128)S(1)} %maximum_convert_fusion, f32[3,32,128]{2,1,0:T(8,128)S(1)} %slice.160), kind=kLoop, calls=%fused_computation.4 | loop fusion | flops 2621440 | bytes 2342912 | tf_op jit(solution)/shard_map/reduce_sum | solution.py:125
  57.4 3.2 %multiply_reduce_fusion = f32[32,128,128]{2,1,0:T(8,128)S(1)} fusion(f32[5,128,128]{2,1,0:T(8,128)S(1)} %fusion.27, f32[5,32,128]{2,1,0:T(8,128)S(1)} %slice.162), kind=kLoop, calls=%fused_computation.2 | loop fusion | flops 4718592 | bytes 2506752 | tf_op jit(solution)/shard_map/reduce_sum | solution.py:125
  60.6 2.4 %fusion = f32[4096,128]{1,0:T(8,128)} fusion(f32[32,128,128]{2,1,0:T(8,128)S(1)} %multiply_reduce_fusion, f32[1,32,128,128]{3,2,0,1:T(8,128)S(1)} %copy-done.6, f32[32,128,128]{2,1,0:T(8,128)S(1)} %multiply_reduce_fusion.2, f32[1,32,128,128]{3,2,0,1:T(8,128)S(1)} %copy-done.7, f32[1,32,128,128]{3,2,0,1:T(8,128)S(1)} %copy-done.5, ...), kind=kLoop, calls=%fused_computation.8 | loop fusion | flops 3145728 | bytes 12664832 | tf_op jit(solution)/shard_map/add | solution.py:129
  63.1 23.0 %scatter_custom_fusion = f32[2304,128]{1,0:T(8,128)S(1)} fusion(s32[4096]{0:T(1024)S(1)} %bitcast.178, f32[4096,128]{1,0:T(8,128)} %fusion, f32[]{:T(128)} %constant.14.clone.1), kind=kCustom, calls=%fused_computation.36 | custom fusion | flops 524288 | bytes 1180160 | tf_op jit(solution)/shard_map/scatter-add | solution.py:134
  86.2 1.7 %collective-permute-start.5 = (f32[1,3,256,128]{3,2,1,0:T(8,128)S(1)}, f32[1,3,256,128]{3,2,1,0:T(8,128)S(1)}, u32[]{:S(2)}, u32[]{:S(2)}) collective-permute-start(f32[1,3,256,128]{3,2,1,0:T(8,128)S(1)} %bitcast.175), channel_id=1, source_target_pairs={{8,0},{16,8},{24,16},{0,24},{9,1},{17,9},{25,17},{1,25},{10,2},{18... | collective-permute-start | bytes 1179656 | tf_op jit(solution)/shard_map/ppermute | solution.py:20
  87.9 1.3 fusion.14
  89.3 0.3 copy-done.4
  89.5 1.3 fusion.17
  90.9 5.9 %collective-permute-done.4 = f32[1,3,256,128]{3,2,1,0:T(8,128)S(1)} collective-permute-done((f32[1,3,256,128]{3,2,1,0:T(8,128)S(1)}, f32[1,3,256,128]{3,2,1,0:T(8,128)S(1)}, u32[]{:S(2)}, u32[]{:S(2)}) %collective-permute-start.4) | collective-permute-done | bytes 393248 | tf_op jit(solution)/shard_map/ppermute | solution.py:18
  96.9 2.5 %collective-permute-start.6 = (f32[1,256,128]{2,1,0:T(8,128)S(1)}, f32[1,256,128]{2,1,0:T(8,128)S(1)}, u32[]{:S(2)}, u32[]{:S(2)}) collective-permute-start(f32[1,256,128]{2,1,0:T(8,128)S(1)} %get-tuple-element.16), channel_id=1, source_target_pairs={{0,1},{1,2},{2,3},{3,4},{4,5},{5,6},{6,7},{7,0},{8,9},{9,10},{10,1... | collective-permute-start | bytes 393224 | tf_op jit(solution)/shard_map/ppermute | solution.py:18
  99.4 1.4 fusion.11
  100.9 43.6 %psum.7 = f32[3,16,128]{2,1,0:T(8,128)} all-reduce(f32[3,16,128]{2,1,0:T(8,128)S(1)} %pad_maximum_fusion.4), channel_id=1, replica_groups=mesh['gz'=4,'xy'=8] {'gz','xy'}, use_global_device_ids=true, to_apply=%region_8.0 | all-reduce | flops 6144 | bytes 49152 | tf_op jit(solution)/shard_map/psum | solution.py:137
  144.5 0.7 fusion.29
  145.2 3.8 %reduce_sum.89 = f32[3,128,128]{2,1,0:T(8,128)} reduce(f32[32,3,128,128]{3,2,1,0:T(8,128)} %bitcast.173, f32[]{:T(128)} %constant.14.clone.1), dimensions={0}, to_apply=%region_9.0 | reduce | flops 1523712 | bytes 6488068 | tf_op jit(solution)/shard_map/reduce_sum | solution.py:120
  (72 shorter events, 1.7 us)
Async XLA Ops:
  7.2 3.6 %copy-start = (f32[3,16,128]{2,1,0:T(8,128)S(1)}, f32[3,16,128]{2,1,0:T(8,128)}, u32[]{:S(2)}) copy-start(f32[3,16,128]{2,1,0:T(8,128)} %param.12) | copy-start | bytes 73732
  7.2 138.0 %all-gather.3.cloned.1.call-start = ((), (), s32[]{:S(2)}) async-start(), calls=%async_computation | async-start | bytes 6488064 | tf_op jit(solution)/shard_map/all_gather | solution.py:120
  7.2 11.7 %collective-permute-start = (bf16[1,1,256,128]{3,2,1,0:T(8,128)(2,1)}, bf16[1,1,256,128]{3,2,1,0:T(8,128)(2,1)S(1)}, u32[]{:S(2)}, u32[]{:S(2)}) collective-permute-start(bf16[1,1,256,128]{3,2,1,0:T(8,128)(2,1)} %param.11), channel_id=1, source_target_pairs={{0,8},{8,16},{16,24},{24,0},{1,9},{9,17},{17,25},{25,1},{2,10},{10... | collective-permute-start | bytes 196616 | tf_op jit(solution)/shard_map/ppermute | solution.py:18
  7.3 11.7 %collective-permute-start.1 = (bf16[1,1,256,128]{3,2,1,0:T(8,128)(2,1)}, bf16[1,1,256,128]{3,2,1,0:T(8,128)(2,1)S(1)}, u32[]{:S(2)}, u32[]{:S(2)}) collective-permute-start(bf16[1,1,256,128]{3,2,1,0:T(8,128)(2,1)} %param.11), channel_id=1, source_target_pairs={{8,0},{16,8},{24,16},{0,24},{9,1},{17,9},{25,17},{1,25},{10,2},{18... | collective-permute-start | bytes 196616 | tf_op jit(solution)/shard_map/ppermute | solution.py:20
  10.7 7.3 %copy-start.9 = (bf16[1,1,9,128,128]{4,3,2,1,0:T(8,128)(2,1)S(1)}, bf16[1,1,9,128,128]{4,3,2,1,0:T(8,128)(2,1)}, u32[]{:S(2)}) copy-start(bf16[1,1,9,128,128]{4,3,2,1,0:T(8,128)(2,1)} %param.7) | copy-start | bytes 884740
  10.7 8.2 %copy-start.11 = (bf16[1,1,256,128]{3,2,1,0:T(8,128)(2,1)S(1)}, bf16[1,1,256,128]{3,2,1,0:T(8,128)(2,1)}, u32[]{:S(2)}) copy-start(bf16[1,1,256,128]{3,2,1,0:T(8,128)(2,1)} %param.11) | copy-start | bytes 196612
  10.7 10.3 %copy-start.12 = (s32[1,1,32,128]{3,2,1,0:T(8,128)S(1)}, s32[1,1,32,128]{3,2,1,0:T(8,128)}, u32[]{:S(2)}) copy-start(s32[1,1,32,128]{3,2,1,0:T(8,128)} %param.9) | copy-start | bytes 49156
  19.0 11.0 %collective-permute-start.2 = (bf16[3,1,256,128]{3,2,1,0:T(8,128)(2,1)S(1)}, bf16[3,1,256,128]{3,2,1,0:T(8,128)(2,1)S(1)}, u32[]{:S(2)}, u32[]{:S(2)}) collective-permute-start(bf16[3,1,256,128]{3,2,1,0:T(8,128)(2,1)S(1)} %constant_dynamic-update-slice_fusion.9), channel_id=1, source_target_pairs={{0,1},{1,2},{2,3},{3,4},{4,5},{5,6},{6,7},{7,0},{8,9},{9,10},{10,1... | collective-permute-start | bytes 589832 | tf_op jit(solution)/shard_map/ppermute | solution.py:18
  20.6 9.4 %collective-permute-start.3 = (bf16[3,1,256,128]{3,2,1,0:T(8,128)(2,1)S(1)}, bf16[3,1,256,128]{3,2,1,0:T(8,128)(2,1)S(1)}, u32[]{:S(2)}, u32[]{:S(2)}) collective-permute-start(bf16[3,1,256,128]{3,2,1,0:T(8,128)(2,1)S(1)} %constant_dynamic-update-slice_fusion.9), channel_id=1, source_target_pairs={{1,0},{2,1},{3,2},{4,3},{5,4},{6,5},{7,6},{0,7},{9,8},{10,9},{11,1... | collective-permute-start | bytes 589832 | tf_op jit(solution)/shard_map/ppermute | solution.py:20
  47.4 2.0 %copy-start.10 = (bf16[3,128,128]{2,1,0:T(8,128)(2,1)S(1)}, bf16[3,128,128]{2,1,0:T(8,128)(2,1)}, u32[]{:S(2)}) copy-start(bf16[3,128,128]{2,1,0:T(8,128)(2,1)} %param.13) | copy-start | bytes 294916
  49.4 3.6 %copy-start.8 = (f32[1,1,9,128,128]{4,3,2,1,0:T(8,128)S(1)}, f32[1,1,9,128,128]{4,3,2,1,0:T(8,128)}, u32[]{:S(2)}) copy-start(f32[1,1,9,128,128]{4,3,2,1,0:T(8,128)} %convert_element_type.43) | copy-start | bytes 1769476
  55.1 5.5 %copy-start.7 = (f32[1,32,128,128]{3,2,0,1:T(8,128)S(1)}, f32[1,32,128,128]{3,2,0,1:T(8,128)}, u32[]{:S(2)}) copy-start(f32[1,32,128,128]{3,2,0,1:T(8,128)} %get-tuple-element.10) | copy-start | bytes 6291460
  55.2 5.4 %copy-start.5 = (f32[1,32,128,128]{3,2,0,1:T(8,128)S(1)}, f32[1,32,128,128]{3,2,0,1:T(8,128)}, u32[]{:S(2)}) copy-start(f32[1,32,128,128]{3,2,0,1:T(8,128)} %get-tuple-element.5) | copy-start | bytes 6291460
  55.2 5.4 %copy-start.6 = (f32[1,32,128,128]{3,2,0,1:T(8,128)S(1)}, f32[1,32,128,128]{3,2,0,1:T(8,128)}, u32[]{:S(2)}) copy-start(f32[1,32,128,128]{3,2,0,1:T(8,128)} %get-tuple-element.9) | copy-start | bytes 6291460
  57.4 5.7 %copy-start.1 = (f32[32,128,128]{2,1,0:T(8,128)}, f32[32,128,128]{2,1,0:T(8,128)S(1)}, u32[]{:S(2)}) copy-start(f32[32,128,128]{2,1,0:T(8,128)S(1)} %multiply_reduce_fusion.2) | copy-start | bytes 6291460
  60.6 2.5 %copy-start.3 = (f32[32,128,128]{2,1,0:T(8,128)}, f32[32,128,128]{2,1,0:T(8,128)S(1)}, u32[]{:S(2)}) copy-start(f32[32,128,128]{2,1,0:T(8,128)S(1)} %multiply_reduce_fusion) | copy-start | bytes 6291460
  86.0 1.9 %copy-start.2 = (f32[32,128,128]{2,1,0:T(8,128)S(1)}, f32[32,128,128]{2,1,0:T(8,128)}, u32[]{:S(2)}) copy-start(f32[32,128,128]{2,1,0:T(8,128)} %copy-done.1) | copy-start | bytes 6291460
  86.1 10.7 %collective-permute-start.4 = (f32[1,3,256,128]{3,2,1,0:T(8,128)S(1)}, f32[1,3,256,128]{3,2,1,0:T(8,128)S(1)}, u32[]{:S(2)}, u32[]{:S(2)}) collective-permute-start(f32[1,3,256,128]{3,2,1,0:T(8,128)S(1)} %bitcast.176), channel_id=1, source_target_pairs={{0,8},{8,16},{16,24},{24,0},{1,9},{9,17},{17,25},{25,1},{2,10},{10... | collective-permute-start | bytes 1179656 | tf_op jit(solution)/shard_map/ppermute | solution.py:18
  86.2 10.6 %collective-permute-start.5 = (f32[1,3,256,128]{3,2,1,0:T(8,128)S(1)}, f32[1,3,256,128]{3,2,1,0:T(8,128)S(1)}, u32[]{:S(2)}, u32[]{:S(2)}) collective-permute-start(f32[1,3,256,128]{3,2,1,0:T(8,128)S(1)} %bitcast.175), channel_id=1, source_target_pairs={{8,0},{16,8},{24,16},{0,24},{9,1},{17,9},{25,17},{1,25},{10,2},{18... | collective-permute-start | bytes 1179656 | tf_op jit(solution)/shard_map/ppermute | solution.py:20
  87.9 1.6 %copy-start.4 = (f32[32,128,128]{2,1,0:T(8,128)S(1)}, f32[32,128,128]{2,1,0:T(8,128)}, u32[]{:S(2)}) copy-start(f32[32,128,128]{2,1,0:T(8,128)} %copy-done.3) | copy-start | bytes 6291460
  96.9 47.6 %collective-permute-start.6 = (f32[1,256,128]{2,1,0:T(8,128)S(1)}, f32[1,256,128]{2,1,0:T(8,128)S(1)}, u32[]{:S(2)}, u32[]{:S(2)}) collective-permute-start(f32[1,256,128]{2,1,0:T(8,128)S(1)} %get-tuple-element.16), channel_id=1, source_target_pairs={{0,1},{1,2},{2,3},{3,4},{4,5},{5,6},{6,7},{7,0},{8,9},{9,10},{10,1... | collective-permute-start | bytes 393224 | tf_op jit(solution)/shard_map/ppermute | solution.py:18
  99.4 45.1 %collective-permute-start.7 = (f32[1,256,128]{2,1,0:T(8,128)S(1)}, f32[1,256,128]{2,1,0:T(8,128)S(1)}, u32[]{:S(2)}, u32[]{:S(2)}) collective-permute-start(f32[1,256,128]{2,1,0:T(8,128)S(1)} %get-tuple-element.17), channel_id=1, source_target_pairs={{1,0},{2,1},{3,2},{4,3},{5,4},{6,5},{7,6},{0,7},{9,8},{10,9},{11,1... | collective-permute-start | bytes 393224 | tf_op jit(solution)/shard_map/ppermute | solution.py:20
Sparse Core Ops, SparseCore 0:
  54.7 74.6 all-gather.2
